TPU v7x, 512 devices: a whole 4x4x16 slice. The times are simulated.
512 devices in a mesh: seq: 64 (over z, y), dp: 8 (over x, core).
Axes of the slice: x: 4, y: 4, z: 16, core: 2. Of those that a mesh axis runs over, the one named last changes fastest.
Arguments:
- phonemes: bfloat16 [32768, 1024], P(('dp', 'seq')), parts along dimension 0, may hold values from -6 to 6
- spread: float32 [32768], P(('dp', 'seq')), parts along dimension 0, may hold values from 2 to 8
- durations: int32 [512, 64], P(('dp', 'seq')), parts along dimension 0, may hold values from 1 to 32, 512 in all within a row
- norm_gain: float32 [1024], replicated, may hold values from 0.1 to 1.9
- w_query: bfloat16 [1024, 1024], P('seq')
- w_key: bfloat16 [1024, 1024], P('seq'), may hold values from -0.1875 to 0.1875
- w_value: bfloat16 [1024, 1024], P('seq'), may hold values from -0.1875 to 0.1875
- w_out: bfloat16 [1024, 1024], P('seq'), may hold values from -0.1875 to 0.1875
Outputs:
- frames_out: bfloat16 [262144, 1024], P(('dp', 'seq')), parts along dimension 0
There are 8 independent parts, one for each index of `dp`. A program takes and returns all parts, laid end to end along the dimension named above; an argument that names none is the same for every part. Nothing has to cross between parts.
Inputs may be any that keep to these rules, and one draw needn't show every extreme that they name: Each row holds the durations of the 64 phonemes of one block of 512 frames: it sums to 512 and its largest entry is 32.
All inputs are finite; a program needn't handle non-finite values.
Results may differ from a plain program's by a relative error of at most 0.035.
Values may be sent and summed in bfloat16 or wider, within the bound.
A program may use at most 128 MiB of HBM per device.

v0:
```python
import math

import jax
import jax.numpy as jnp
from jax import lax
from jax.sharding import PartitionSpec as P

HEADS = 16
HEAD_DIM = 64
FR_DEV = 512
RADIUS = 32
WIN = 128


def extended(array, sides, width):
    for axis, dim in sides:
        count, length = (lax.axis_size(axis), array.shape[dim])
        up = [(i, (i + 1) % count) for i in range(count - 1)]
        down = [(j, i) for i, j in up]
        last = lax.slice_in_dim(array, length - width, length, axis=dim)
        initial = lax.slice_in_dim(array, 0, width, axis=dim)
        before = lax.ppermute(last, axis, up)
        after = lax.ppermute(initial, axis, down)
        array = jnp.concatenate([before, array, after], axis=dim)
    return array


def band_weights(frame_pos, centers, spread, usable):
    offset = frame_pos[:, None] - centers[None, :]
    sigma = jnp.where(usable, spread, 1.0)
    inside = usable[None, :] & (jnp.abs(offset) <= RADIUS)
    return jnp.where(inside, jnp.exp(-(offset * offset) / (2.0 * sigma * sigma)[None, :]), 0.0)


def attend(query, keys, values, allowed):
    row_count = query.shape[0]
    key_count = keys.shape[0]
    q_heads = query.reshape(row_count, HEADS, HEAD_DIM)
    k_heads = keys.reshape(key_count, HEADS, HEAD_DIM)
    v_heads = values.reshape(key_count, HEADS, HEAD_DIM)
    scores = jnp.einsum("thd,uhd->htu", q_heads, k_heads, preferred_element_type=jnp.float32) * (
        1.0 / math.sqrt(HEAD_DIM)
    )
    scores = jnp.where(allowed[None], scores, -1e30)
    row_max = jnp.max(scores, axis=2, keepdims=True)
    raised = jnp.exp(scores - row_max)
    weights_bf = (raised / jnp.sum(raised, axis=2, keepdims=True)).astype(jnp.bfloat16)
    mixture = jnp.einsum("htu,uhd->thd", weights_bf, v_heads, preferred_element_type=jnp.float32)
    return mixture.reshape(row_count, HEADS * HEAD_DIM).astype(jnp.bfloat16)


def on_device(phonemes, spread, durations, norm_gain, w_query, w_key, w_value, w_out):
    seq_count = lax.axis_size("seq")
    my_index = lax.axis_index("seq")
    ph_count = phonemes.shape[0]
    dur_row = durations[0]
    end_frames = jnp.cumsum(dur_row) + my_index * FR_DEV
    centers = end_frames.astype(jnp.float32) - dur_row.astype(jnp.float32) * 0.5
    wide_rows, wide_centers, wide_spread = (
        extended(phonemes.astype(jnp.float32), (("seq", 0),), RADIUS),
        extended(centers, (("seq", 0),), RADIUS),
        extended(spread, (("seq", 0),), RADIUS),
    )
    slot_ids = jnp.arange(ph_count + 2 * RADIUS, dtype=jnp.int32)
    usable = ((slot_ids >= RADIUS) | (my_index > 0)) & (
        (slot_ids < ph_count + RADIUS) | (my_index < seq_count - 1)
    )
    frame_pos = (my_index * FR_DEV + jnp.arange(FR_DEV, dtype=jnp.int32)).astype(jnp.float32) + 0.5
    band = band_weights(frame_pos, wide_centers, wide_spread, usable)
    totals = jnp.sum(band, axis=1)
    upsampled = (
        jnp.dot(
            band.astype(jnp.bfloat16),
            wide_rows.astype(jnp.bfloat16),
            preferred_element_type=jnp.float32,
        )
        / totals[:, None]
    ).astype(jnp.bfloat16)
    wide_f32 = upsampled.astype(jnp.float32)
    normed = (
        wide_f32
        * lax.rsqrt(jnp.mean(wide_f32 * wide_f32, axis=1, keepdims=True) + 1e-06)
        * norm_gain
    ).astype(jnp.bfloat16)
    full_query, full_key, full_value, full_out = (
        lax.all_gather(w_query, "seq", axis=0, tiled=True),
        lax.all_gather(w_key, "seq", axis=0, tiled=True),
        lax.all_gather(w_value, "seq", axis=0, tiled=True),
        lax.all_gather(w_out, "seq", axis=0, tiled=True),
    )
    query = jnp.dot(normed, full_query, preferred_element_type=jnp.float32).astype(jnp.bfloat16)
    key_rows = jnp.dot(normed, full_key, preferred_element_type=jnp.float32).astype(jnp.bfloat16)
    value_rows = jnp.dot(normed, full_value, preferred_element_type=jnp.float32).astype(
        jnp.bfloat16
    )
    wide_keys, wide_values = (
        extended(key_rows, (("seq", 0),), WIN),
        extended(value_rows, (("seq", 0),), WIN),
    )
    frames_all = FR_DEV * seq_count
    q_pos = my_index * FR_DEV + jnp.arange(FR_DEV, dtype=jnp.int32)
    k_pos = my_index * FR_DEV - WIN + jnp.arange(FR_DEV + 2 * WIN, dtype=jnp.int32)
    allowed = (
        (k_pos >= 0)[None, :]
        & (k_pos < frames_all)[None, :]
        & (jnp.abs(q_pos[:, None] - k_pos[None, :]) <= WIN)
    )
    attended = attend(query, wide_keys, wide_values, allowed)
    projected = jnp.dot(attended, full_out, preferred_element_type=jnp.float32)
    return (wide_f32 + projected).astype(jnp.bfloat16)


def solution(mesh):
    placed = (
        P(("dp", "seq"), None),
        P(("dp", "seq")),
        P(("dp", "seq"), None),
        P(),
        P("seq", None),
        P("seq", None),
        P("seq", None),
        P("seq", None),
    )
    return jax.shard_map(
        on_device, mesh=mesh, in_specs=placed, out_specs=P(("dp", "seq"), None), check_vma=False
    )
```

profile of v0, /device:TPU:1, one launch (start us, length us, event | category | flops | bytes accessed | tf_op | source)
XLA Modules:
  0.0 578.1 jit_solution(6542820790243993728)
XLA Ops:
  6.5 0.0 all-gather.9.cloned.1.call-start
  6.5 0.7 all-gather.9.cloned.1.call-update
  7.3 0.0 all-gather.5.cloned.1.call-start
  7.3 0.7 all-gather.5.cloned.1.call-update
  8.0 0.0 all-gather.7.cloned.1.call-start
  8.1 0.7 all-gather.7.cloned.1.call-update
  8.7 0.0 all-gather.11.cloned.1.call-start
  8.8 0.7 copy.17
  9.5 0.1 reduce-window.9
  9.6 0.1 convert_reduce_fusion
  9.7 0.7 bitcast_subtract_fusion
  10.4 0.1 fusion.39
  10.5 4.0 collective-permute-start
  14.5 1.3 collective-permute-start.1
  15.8 0.8 fusion.40
  16.6 4.0 collective-permute-start.2
  20.6 1.3 collective-permute-start.3
  21.9 0.9 fusion.38
  22.8 4.0 collective-permute-start.4
  26.8 0.0 all-gather.11.cloned.1.call-update
  26.9 0.5 fusion.10
  27.4 0.0 collective-permute-done
  27.4 1.3 collective-permute-start.5
  28.7 0.0 collective-permute-done.1
  28.7 0.1 pad_maximum_fusion.2
  28.8 0.0 collective-permute-done.2
  28.8 0.0 collective-permute-done.3
  28.8 0.7 multiply_multiply_fusion
  29.5 0.3 fusion.24
  29.8 0.0 collective-permute-done.4
  29.8 2.6 collective-permute-done.5
  32.4 1.5 fusion.6
  33.9 113.8 %all-gather.9.cloned.1.call-done = bf16[1024,1024]{1,0:T(8,128)(2,1)} async-done(((bf16[16,1024]{1,0:T(8,128)(2,1)}), bf16[1024,1024]{1,0:T(8,128)(2,1)}) %all-gather.9.cloned.1.call-update) | async-done | bytes 2097168 | tf_op jit(solution)/shard_map/all_gather | solution.py:87
  147.8 0.0 copy-done.5
  147.8 0.0 copy-done.4
  147.8 2.9 convolution_convert_fusion
  150.7 1.7 collective-permute-start.8
  152.4 1.3 collective-permute-start.9
  153.7 134.0 %all-gather.5.cloned.1.call-done = bf16[1024,1024]{1,0:T(8,128)(2,1)} async-done(((bf16[16,1024]{1,0:T(8,128)(2,1)}), bf16[1024,1024]{1,0:T(8,128)(2,1)}) %all-gather.5.cloned.1.call-update) | async-done | bytes 2097168 | tf_op jit(solution)/shard_map/all_gather | solution.py:88
  287.7 3.2 convolution_convert_fusion.2
  290.9 0.0 copy-start
  290.9 1.0 copy-done
  291.9 0.8 fusion.37
  292.7 1.7 collective-permute-start.6
  294.4 1.5 collective-permute-start.7
  295.9 131.7 %all-gather.7.cloned.1.call-done = bf16[1024,1024]{1,0:T(8,128)(2,1)} async-done(((bf16[16,1024]{1,0:T(8,128)(2,1)}), bf16[1024,1024]{1,0:T(8,128)(2,1)}) %all-gather.7.cloned.1.call-update) | async-done | bytes 2097168 | tf_op jit(solution)/shard_map/all_gather | solution.py:86
  427.7 3.2 convolution_convert_fusion.1
  430.9 1.4 copy.19
  432.2 0.0 collective-permute-done.8
  432.2 0.0 collective-permute-done.9
  432.3 1.1 pad_maximum_fusion.1
  433.3 0.0 copy-start.1
  433.3 1.6 copy.20
  434.9 0.0 collective-permute-done.6
  434.9 0.0 collective-permute-done.7
  434.9 0.0 copy-done.1
  434.9 1.1 pad_maximum_fusion
  436.0 0.0 copy-start.2
  436.0 1.6 copy.18
  437.6 0.0 copy-done.2
  437.6 15.4 %fusion.41 = (f32[16,512]{1,0:T(8,128)}, f32[16,512,768]{2,1,0:T(8,128)}) fusion(pred[512,768]{1,0:T(8,128)(4,1)S(1)} %fusion.10, bf16[512,16,64]{0,2,1:T(8,128)(2,1)} %bitcast.21, bf16[768,16,64]{0,2,1:T(8,128)(2,1)S(1)} %bitcast.19), kind=kOutput, calls=%fused_computation.62 | convolution fusion | flops 830472960 | bytes 28213248 | tf_op jit(solution)/shard_map/sub | solution.py:46
  453.0 10.3 %fusion.11 = bf16[16,64,512]{2,1,0:T(8,128)(2,1)S(1)} fusion(bf16[768,16,64]{0,2,1:T(8,128)(2,1)S(1)} %bitcast.20, f32[16,512,768]{2,1,0:T(8,128)} %get-tuple-element.20, f32[16,512]{1,0:T(8,128)} %get-tuple-element.19), kind=kOutput, calls=%fused_computation.21 | convolution fusion | flops 818413568 | bytes 27820032 | tf_op jit(solution)/shard_map/htu,uhd->thd/dot_general | solution.py:48
  463.3 104.2 %all-gather.11.cloned.1.call-done = bf16[1024,1024]{1,0:T(8,128)(2,1)} async-done(((bf16[16,1024]{1,0:T(8,128)(2,1)}), bf16[1024,1024]{1,0:T(8,128)(2,1)}) %all-gather.11.cloned.1.call-update) | async-done | bytes 2097168 | tf_op jit(solution)/shard_map/all_gather | solution.py:89
  567.5 4.1 fusion.9
  (10 shorter events, 0.1 us)
Async XLA Ops:
  6.5 141.2 %all-gather.9.cloned.1.call-start = ((), (), s32[]{:S(2)}) async-start(), calls=%async_computation.2 | async-start | bytes 2129920 | tf_op jit(solution)/shard_map/all_gather | solution.py:87
  7.3 280.5 %all-gather.5.cloned.1.call-start = ((), (), s32[]{:S(2)}) async-start(), calls=%async_computation | async-start | bytes 2129920 | tf_op jit(solution)/shard_map/all_gather | solution.py:88
  8.0 419.7 %all-gather.7.cloned.1.call-start = ((), (), s32[]{:S(2)}) async-start(), calls=%async_computation.1 | async-start | bytes 2129920 | tf_op jit(solution)/shard_map/all_gather | solution.py:86
  8.7 558.7 %all-gather.11.cloned.1.call-start = ((), (), s32[]{:S(2)}) async-start(), calls=%async_computation.3 | async-start | bytes 2129920 | tf_op jit(solution)/shard_map/all_gather | solution.py:89
  10.5 16.9 %collective-permute-start = (f32[32]{0:T(128)S(1)}, f32[32]{0:T(128)S(1)}, u32[]{:S(2)}, u32[]{:S(2)}) collective-permute-start(f32[32]{0:T(128)S(1)} %get-tuple-element.13), channel_id=1, source_target_pairs={{0,8},{8,16},{16,24},{24,32},{32,40},{40,48},{48,56},{56,64},{64,7... | collective-permute-start | bytes 392 | tf_op jit(solution)/shard_map/ppermute | solution.py:22
  14.5 14.2 %collective-permute-start.1 = (f32[32]{0:T(128)S(1)}, f32[32]{0:T(128)S(1)}, u32[]{:S(2)}, u32[]{:S(2)}) collective-permute-start(f32[32]{0:T(128)S(1)} %get-tuple-element.14), channel_id=1, source_target_pairs={{8,0},{16,8},{24,16},{32,24},{40,32},{48,40},{56,48},{64,56},{72,6... | collective-permute-start | bytes 392 | tf_op jit(solution)/shard_map/ppermute | solution.py:23
  16.6 12.2 %collective-permute-start.2 = (f32[32]{0:T(128)S(1)}, f32[32]{0:T(128)S(1)}, u32[]{:S(2)}, u32[]{:S(2)}) collective-permute-start(f32[32]{0:T(128)S(1)} %get-tuple-element.15), channel_id=1, source_target_pairs={{0,8},{8,16},{16,24},{24,32},{32,40},{40,48},{48,56},{56,64},{64,7... | collective-permute-start | bytes 392 | tf_op jit(solution)/shard_map/ppermute | solution.py:22
  20.6 8.2 %collective-permute-start.3 = (f32[32]{0:T(128)S(1)}, f32[32]{0:T(128)S(1)}, u32[]{:S(2)}, u32[]{:S(2)}) collective-permute-start(f32[32]{0:T(128)S(1)} %get-tuple-element.16), channel_id=1, source_target_pairs={{8,0},{16,8},{24,16},{32,24},{40,32},{48,40},{56,48},{64,56},{72,6... | collective-permute-start | bytes 392 | tf_op jit(solution)/shard_map/ppermute | solution.py:23
  22.8 7.0 %collective-permute-start.4 = (bf16[32,1024]{1,0:T(8,128)(2,1)S(1)}, bf16[32,1024]{1,0:T(8,128)(2,1)S(1)}, u32[]{:S(2)}, u32[]{:S(2)}) collective-permute-start(bf16[32,1024]{1,0:T(8,128)(2,1)S(1)} %get-tuple-element.11), channel_id=1, source_target_pairs={{0,8},{8,16},{16,24},{24,32},{32,40},{40,48},{48,56},{56,64},{64,7... | collective-permute-start | bytes 196616 | tf_op jit(solution)/shard_map/ppermute | solution.py:22
  27.4 5.0 collective-permute-start.5
  29.8 118.0 %copy-start.4 = (f32[1024]{0:T(1024)S(1)}, f32[1024]{0:T(1024)}, u32[]{:S(2)}) copy-start(f32[1024]{0:T(1024)} %param.11) | copy-start | bytes 12292
  33.9 113.8 %copy-start.5 = (bf16[512,1024]{1,0:T(8,128)(2,1)}, bf16[512,1024]{1,0:T(8,128)(2,1)S(1)}, u32[]{:S(2)}) copy-start(bf16[512,1024]{1,0:T(8,128)(2,1)S(1)} %get-tuple-element.18) | copy-start | bytes 3145732
  150.7 281.5 %collective-permute-start.8 = (bf16[128,1024]{1,0:T(8,128)(2,1)S(1)}, bf16[128,1024]{1,0:T(8,128)(2,1)S(1)}, u32[]{:S(2)}, u32[]{:S(2)}) collective-permute-start(bf16[128,1024]{1,0:T(8,128)(2,1)S(1)} %get-tuple-element.7), channel_id=1, source_target_pairs={{0,8},{8,16},{16,24},{24,32},{32,40},{40,48},{48,56},{56,64},{64,7... | collective-permute-start | bytes 786440 | tf_op jit(solution)/shard_map/ppermute | solution.py:22
  152.4 279.8 %collective-permute-start.9 = (bf16[128,1024]{1,0:T(8,128)(2,1)S(1)}, bf16[128,1024]{1,0:T(8,128)(2,1)}, u32[]{:S(2)}, u32[]{:S(2)}) collective-permute-start(bf16[128,1024]{1,0:T(8,128)(2,1)S(1)} %get-tuple-element.8), channel_id=1, source_target_pairs={{8,0},{16,8},{24,16},{32,24},{40,32},{48,40},{56,48},{64,56},{72,6... | collective-permute-start | bytes 786440 | tf_op jit(solution)/shard_map/ppermute | solution.py:23
  290.9 1.0 copy-start
  292.7 142.2 %collective-permute-start.6 = (bf16[128,1024]{1,0:T(8,128)(2,1)}, bf16[128,1024]{1,0:T(8,128)(2,1)S(1)}, u32[]{:S(2)}, u32[]{:S(2)}) collective-permute-start(bf16[128,1024]{1,0:T(8,128)(2,1)} %get-tuple-element.9), channel_id=1, source_target_pairs={{0,8},{8,16},{16,24},{24,32},{32,40},{40,48},{48,56},{56,64},{64,7... | collective-permute-start | bytes 786440 | tf_op jit(solution)/shard_map/ppermute | solution.py:22
  294.4 140.5 %collective-permute-start.7 = (bf16[128,1024]{1,0:T(8,128)(2,1)}, bf16[128,1024]{1,0:T(8,128)(2,1)}, u32[]{:S(2)}, u32[]{:S(2)}) collective-permute-start(bf16[128,1024]{1,0:T(8,128)(2,1)} %get-tuple-element.10), channel_id=1, source_target_pairs={{8,0},{16,8},{24,16},{32,24},{40,32},{48,40},{56,48},{64,56},{72,6... | collective-permute-start | bytes 786440 | tf_op jit(solution)/shard_map/ppermute | solution.py:23
  433.3 1.6 copy-start.1
  436.0 1.6 copy-start.2
  437.6 15.4 %copy-start.3 = (bf16[768,1024]{0,1:T(8,128)(2,1)S(1)}, bf16[768,1024]{0,1:T(8,128)(2,1)}, u32[]{:S(2)}) copy-start(bf16[768,1024]{0,1:T(8,128)(2,1)} %copy.18) | copy-start | bytes 4718596
Sparse Core Ops, SparseCore 0:
  10.3 137.4 all-gather.8
  150.7 136.9 all-gather.4
  290.7 136.9 all-gather.6
  430.5 136.9 all-gather.10
where the time goes:
time: 587 us; the launch traced here: 578 us
  waiting for transfers between devices  488 us (83%)
  matrix products  40.6 us (7%)
  starting transfers between devices  22.1 us (4%)
  between operations  13.4 us (2%)
  local copies, waits for them, and re-layouts  8.91 us (2%)
    all_gather x1, waiting for transfers between devices, on_device(): lax.all_gather(w_value, 'seq', axis=0, tiled=True)  134 us
    all_gather x1, waiting for transfers between devices, on_device(): lax.all_gather(w_query, 'seq', axis=0, tiled=True)  132 us
    all_gather x1, waiting for transfers between devices, on_device(): lax.all_gather(w_key, 'seq', axis=0, tiled=True)  114 us
    all_gather x1, waiting for transfers between devices, on_device(): lax.all_gather(w_out, 'seq', axis=0, tiled=True)  104 us
    sub x1, matrix products, attend(): raised = jnp.exp(scores - row_max)  15.4 us
    ppermute x5, starting transfers between devices, extended(): before = lax.ppermute(last, axis, up)  15.3 us
  transfers between devices with their start and end apart: 14, of which 5 were waited for; matrix products, arithmetic and copies ran while one was open for 8% of the time, Pallas kernels for 0%

commit v1 on v0

v1 whole, which is shorter than its diff:
```python
import functools
import math

import jax
import jax.numpy as jnp
from jax import lax
from jax.experimental import pallas as pl
from jax.experimental.pallas import tpu as pltpu
from jax.sharding import PartitionSpec as P

MESH = pl.DeviceIdType.MESH
NZ, NY, NX = 16, 4, 4
D = 1024
FR = 512
PH = 64
RADIUS = 32.0
WIN = 128
KEYS = FR + 2 * WIN
BLK = 128
SPAN = BLK + 2 * WIN
GROUP = 256
SCALE = math.log2(math.e) / 8.0
VAL, QRY, KEY, OUT = 0, 1, 2, 3


def kernel(ph, spread, dur, gain, w_val, w_qry, w_key, w_out, out,
           full, phx, aux, auxs, up, qs, ks, vs, att,
           zs, zr, ms, mr, ls, lr, cs, cr, own, hs, hr, asem, arem):
    s = lax.axis_index("seq")
    d = lax.axis_index("dp")
    z, y, x, c = s // NY, s % NY, d // 2, d % 2
    shards = (w_val, w_qry, w_key, w_out)

    def at(dz, dy, dx, dc):
        zz, yy, xx, cc = (z + dz) % NZ, (y + dy) % NY, (x + dx) % NX, (c + dc) % 2
        return (zz * NY + yy, xx * 2 + cc)

    after = ((s + 1) % (NZ * NY), d)
    before = ((s + NZ * NY - 1) % (NZ * NY), d)

    barrier = pltpu.get_barrier_semaphore()

    def greet(dev):
        pl.semaphore_signal(barrier, inc=1, device_id=dev, device_id_type=MESH)

    for k in range(1, NZ):
        greet(at(k, 0, 0, 0))
    for k in range(1, NY):
        greet(at(0, k, 0, 0))
        greet(at(0, 0, k, 0))
    greet(at(0, 0, 0, 1))
    greet(after)
    greet(before)

    durf = dur[...].astype(jnp.float32)
    row = lax.broadcasted_iota(jnp.int32, (PH, PH), 0)
    col = lax.broadcasted_iota(jnp.int32, (PH, PH), 1)
    tri = jnp.where(row <= col, 1.0, 0.0).astype(jnp.bfloat16)
    ends = jnp.dot(jnp.broadcast_to(durf, (8, PH)).astype(jnp.bfloat16), tri,
                   preferred_element_type=jnp.float32)
    auxs[...] = jnp.zeros_like(auxs)
    auxs[0:1, 0:PH] = ends[0:1] - durf * 0.5
    auxs[1:2, 0:PH] = spread[...]

    pl.semaphore_wait(barrier, (NZ - 1) + (NY - 1) + (NX - 1) + 1 + 2)

    def remote(src, dst, ssem, rsem, dev):
        return pltpu.make_async_remote_copy(
            src_ref=src, dst_ref=dst, send_sem=ssem, recv_sem=rsem, device_id=dev, device_id_type=MESH)

    def waited(ref, sem):
        pltpu.make_async_copy(ref, ref, sem).wait()

    remote(auxs, aux.at[0], asem.at[0], arem.at[0], after).start()
    remote(auxs, aux.at[2], asem.at[1], arem.at[1], before).start()
    remote(ph, phx.at[0], hs.at[0], hr.at[0], after).start()
    remote(ph, phx.at[2], hs.at[1], hr.at[1], before).start()

    columns = pl.ds(pl.multiple_of(d * 128, 128), 128)
    for w in range(4):
        piece = shards[w].at[:, columns]
        pltpu.make_async_copy(piece, full.at[w, x, c, z, y], own.at[w]).start()

        def send_z(j, carry, w=w, piece=piece):
            half = (j + 1) // 2
            k = 8 + half * (1 - 2 * (j % 2))
            remote(piece, full.at[w, x, c, z, y], zs.at[w], zr.at[w], at(k, 0, 0, 0)).start()
            return carry

        lax.fori_loop(0, NZ - 1, send_z, 0)
    pltpu.make_async_copy(ph, phx.at[1], own.at[4]).start()
    aux[1] = auxs[...]

    def mid(w):
        pltpu.make_async_copy(shards[w].at[:, columns], full.at[w, x, c, z, y], own.at[w]).wait()
        waited(full.at[w, x, c, pl.ds(0, NZ - 1), 0], zr.at[w])
        for k in (2, 1, 3):
            remote(full.at[w, x, c, :, y], full.at[w, x, c, :, y], ms.at[w], mr.at[w],
                   at(0, k * (1 - c), k * c, 0)).start()

    def portion(w, cc, k):
        if cc == 0:
            return full.at[w, (x + NX - k) % NX, 0]
        return full.at[w, :, 1, :, (y + NY - k) % NY]

    def each_core(body):
        for cc in range(2):
            pl.when(c == cc)(functools.partial(body, cc))

    def last(w):
        waited(full.at[w, x, c, pl.ds(0, 12)], mr.at[w])

        def body(cc):
            mine = portion(w, cc, 0)
            for k in (1, 3, 2):
                remote(mine, mine, ls.at[w], lr.at[w * 3 + k - 1],
                       at(0, k * cc, k * (1 - cc), 0)).start()
            remote(mine, mine, cs.at[w], cr.at[w], at(0, 0, 0, 1)).start()

        each_core(body)

    def swap(w):
        def body(cc):
            for k in (1, 3, 2):
                got = portion(w, cc, k)
                waited(got, lr.at[w * 3 + k - 1])
                remote(got, got, cs.at[w], cr.at[w], at(0, 0, 0, 1)).start()

        each_core(body)

    def whole(w):
        waited(full.at[w, :, 0], cr.at[w])

    def weight(w, g):
        return jnp.concatenate(
            [full[w, g, 0].reshape(D, 128), full[w, g, 1].reshape(D, 128)], axis=1)

    waited(aux.at[0], arem.at[0])
    waited(aux.at[2], arem.at[1])
    cent = jnp.concatenate(
        [aux[0, 0:1, 0:PH] - FR, aux[1, 0:1, 0:PH], aux[2, 0:1, 0:PH] + FR], axis=1)
    sig = jnp.concatenate(
        [aux[0, 1:2, 0:PH], aux[1, 1:2, 0:PH], aux[2, 1:2, 0:PH]], axis=1)
    slot = lax.broadcasted_iota(jnp.int32, (1, 3 * PH), 1)
    usable = ((slot >= PH) | (s > 0)) & ((slot < 2 * PH) | (s < NZ * NY - 1))
    reach = jnp.where(usable, RADIUS, -1.0)
    fall = -0.5 / (sig * sig)
    frame = lax.broadcasted_iota(jnp.int32, (KEYS, 3 * PH), 0).astype(jnp.float32) + (0.5 - WIN)
    gap = frame - cent
    band = jnp.where(jnp.abs(gap) <= reach, jnp.exp(gap * gap * fall), 0.0)
    total = jnp.sum(band, axis=1, keepdims=True)
    inv = jnp.where(total > 1e-16, 1.0 / total, 0.0)
    band_bf = band.astype(jnp.bfloat16)
    mid(0)
    waited(phx.at[0], hr.at[0])
    waited(phx.at[2], hr.at[1])
    pltpu.make_async_copy(ph, phx.at[1], own.at[4]).wait()
    rows = phx[...].reshape(3 * PH, D)
    lifted = (jnp.dot(band_bf, rows, preferred_element_type=jnp.float32) * inv).astype(jnp.bfloat16)
    up[...] = lifted[WIN:WIN + FR]
    wide = lifted.astype(jnp.float32)
    norm = lax.rsqrt(jnp.mean(wide * wide, axis=1, keepdims=True) + 1e-6) * inv
    gained = (rows.astype(jnp.float32) * gain[...]).astype(jnp.bfloat16)

    mid(1)
    last(0)
    mid(2)
    last(1)
    mid(3)
    last(2)
    last(3)

    def project(w, band_rows, scale, dest):
        for g in range(4):
            part = jnp.dot(gained, weight(w, g), preferred_element_type=jnp.float32).astype(jnp.bfloat16)
            dest[:, g * GROUP:(g + 1) * GROUP] = (
                jnp.dot(band_rows, part, preferred_element_type=jnp.float32) * scale).astype(jnp.bfloat16)

    swap(0)
    whole(0)
    project(VAL, band_bf, norm, vs)
    swap(1)
    whole(1)
    project(QRY, band_bf[WIN:WIN + FR], norm[WIN:WIN + FR] * SCALE, qs)
    swap(2)
    whole(2)
    project(KEY, band_bf, norm, ks)

    t_id = lax.broadcasted_iota(jnp.int32, (BLK, BLK), 0)
    u_id = lax.broadcasted_iota(jnp.int32, (BLK, BLK), 1)
    lane = lax.broadcasted_iota(jnp.int32, (BLK, GROUP), 1) // 64
    low = -1e30
    for g in range(4):
        if g == 2:
            swap(3)
        lanes = slice(g * GROUP, (g + 1) * GROUP)
        for b in range(4):
            q4 = qs[b * BLK:(b + 1) * BLK, lanes]
            k4 = ks[b * BLK:b * BLK + SPAN, lanes]
            v4 = vs[b * BLK:b * BLK + SPAN, lanes]
            head = u_id >= t_id
            tail = u_id <= t_id
            if b == 0:
                head = head & (s > 0)
            if b == 3:
                tail = tail & (s < NZ * NY - 1)
            head = jnp.where(head, 0.0, low)
            tail = jnp.where(tail, 0.0, low)
            stacked = jnp.concatenate([jnp.where(lane == h, q4, jnp.zeros_like(q4)) for h in range(4)], axis=0)
            scores = lax.dot_general(stacked, k4, (((1,), (1,)), ((), ())), preferred_element_type=jnp.float32)
            bias = jnp.concatenate([head, jnp.zeros((BLK, BLK), jnp.float32), tail], axis=1)
            scores = scores + jnp.concatenate([bias] * 4, axis=0)
            raised = jnp.exp2(scores - jnp.max(scores, axis=1, keepdims=True))
            scale = 1.0 / jnp.sum(raised, axis=1, keepdims=True)
            mixed = jnp.dot(raised.astype(jnp.bfloat16), v4, preferred_element_type=jnp.float32) * scale
            got = jnp.zeros((BLK, GROUP), jnp.float32)
            for h in range(4):
                got = jnp.where(lane == h, mixed[h * BLK:(h + 1) * BLK], got)
            att[b * BLK:(b + 1) * BLK, lanes] = got.astype(jnp.bfloat16)

    whole(3)
    for g in range(4):
        lanes = slice(g * GROUP, (g + 1) * GROUP)
        out[:, lanes] = (
            jnp.dot(att[...], weight(OUT, g), preferred_element_type=jnp.float32)
            + up[:, lanes].astype(jnp.float32)).astype(jnp.bfloat16)

    for i in range(2):
        waited(auxs, asem.at[i])
        waited(ph, hs.at[i])
    for w in range(4):
        waited(full.at[w, x, c, pl.ds(0, NZ - 1), 0], zs.at[w])
        waited(full.at[w, x, c, pl.ds(0, 12)], ms.at[w])
        waited(full.at[w, pl.ds(0, 3), c], ls.at[w])
        waited(full.at[w, :, c], cs.at[w])


def on_device(phonemes, spread, durations, norm_gain, w_query, w_key, w_value, w_out):
    vmem = pl.BlockSpec(memory_space=pltpu.VMEM)
    hbm = pl.BlockSpec(memory_space=pl.ANY)
    bf = jnp.bfloat16
    dma = pltpu.SemaphoreType.DMA
    return pl.pallas_call(
        kernel,
        out_shape=jax.ShapeDtypeStruct((FR, D), bf),
        in_specs=[hbm, vmem, vmem, vmem, hbm, hbm, hbm, hbm],
        out_specs=vmem,
        scratch_shapes=[
            pltpu.VMEM((4, NX, 2, NZ, NY, 16, 128), bf),
            pltpu.VMEM((3, PH, D), bf),
            pltpu.VMEM((3, 8, 128), jnp.float32),
            pltpu.VMEM((8, 128), jnp.float32),
            pltpu.VMEM((FR, D), bf),
            pltpu.VMEM((FR, D), bf),
            pltpu.VMEM((KEYS, D), bf),
            pltpu.VMEM((KEYS, D), bf),
            pltpu.VMEM((FR, D), bf),
            dma((4,)), dma((4,)), dma((4,)), dma((4,)), dma((4,)), dma((12,)),
            dma((4,)), dma((4,)), dma((5,)), dma((2,)), dma((2,)), dma((2,)), dma((2,)),
        ],
        compiler_params=pltpu.CompilerParams(
            collective_id=0, has_side_effects=True, vmem_limit_bytes=56 * 1024 * 1024),
        name="chapter_block",
    )(phonemes, spread.reshape(1, PH), durations, norm_gain.reshape(1, D),
      w_value, w_query, w_key, w_out)


def solution(mesh):
    placed = (
        P(("dp", "seq"), None),
        P(("dp", "seq")),
        P(("dp", "seq"), None),
        P(),
        P("seq", None),
        P("seq", None),
        P("seq", None),
        P("seq", None),
    )
    return jax.shard_map(
        on_device, mesh=mesh, in_specs=placed, out_specs=P(("dp", "seq"), None), check_vma=False
    )
```

time: 587 us -> 71.9 us (0.12); the launches traced: 578 us -> 71.7 us
  waiting for transfers between devices: 488 us -> 0 us
  Pallas kernels: 0 us -> 69.5 us
  matrix products: 40.6 us -> 0 us
  starting transfers between devices: 22.1 us -> 0 us
  between operations: 13.4 us -> 0.01 us
  local copies, waits for them, and re-layouts: 8.91 us -> 2.26 us
    all_gather x4 -> x0, waiting for transfers between devices: 484 us -> none  [the longest x1 134 us: on_device(): lax.all_gather(w_value, 'seq', axis=0, tiled=True)]
    pallas_call x0 -> x1, Pallas kernels: none -> 69.5 us  [on_device(): pl.pallas_call(kernel, out_shape=jax.ShapeDtypeStruct((FR, D), bf), in_sp...]
    dot_general x6 -> x0, matrix products: 25.2 us -> none  [the longest x1 10.3 us: attend(): jnp.einsum('htu,uhd->thd', weights_bf, v_heads, preferred_element_type=jn...]
    ppermute x10 -> x0, starting transfers between devices: 22 us -> none  [the longest x5 15.3 us: extended(): before = lax.ppermute(last, axis, up)]
    sub x1 -> x0, matrix products: 15.4 us -> none  [attend(): raised = jnp.exp(scores - row_max)]
  transfers between devices with their start and end apart: 14 -> 0, of which waited for: 5 -> 0; matrix products, arithmetic and copies ran while one was open for 8% -> 0% of each run, Pallas kernels for 0% -> 0%
where the time goes in v1:
time: 71.9 us; the launch traced here: 71.7 us
  Pallas kernels  69.5 us (97%)
  local copies, waits for them, and re-layouts  2.26 us (3%)
    pallas_call x1, Pallas kernels, on_device(): pl.pallas_call(kernel, out_shape=jax.ShapeDtypeStruct((FR, D), bf), in_sp...  69.5 us
    unnamed x1, local copies, waits for them, and re-layouts  2.26 us

profile of v1, /device:TPU:1, one launch (start us, length us, event | category | flops | bytes accessed | tf_op | source)
XLA Modules:
  0.0 71.7 jit_solution(1038549610663027923)
XLA Ops:
  0.0 69.5 %chapter_block.1 = bf16[512,1024]{1,0:T(8,128)(2,1)} custom-call(bf16[64,1024]{1,0:T(8,128)(2,1)} %ph.1, f32[1,64]{1,0:T(1,128)} %bitcast.3, s32[1,64]{1,0:T(1,128)} %dur.1, f32[1,1024]{1,0:T(1,128)} %bitcast.2, bf16[16,1024]{1,0:T(8,128)(2,1)} %w_val.1, bf16[16,1024]{1,0:T(8,128)(2,1)} %w_qry.1, bf16[16,1024]{1,0:T(8,128)(2,1)} %w_key.1, bf16[16,1024]{1,0:T(8,128)(2,1)} %w_out.1), custom_call_target="tpu_custom_call" | custom-call | tf_op jit(solution)/shard_map/chapter_block/pallas_call | solution.py:243
  69.5 2.3 %copy.10 = bf16[512,1024]{1,0:T(8,128)(2,1)} copy(bf16[512,1024]{1,0:T(8,128)(2,1)} %chapter_block.1) | data formatting | bytes 2097152

commit v2 on v1

v2 whole, which is shorter than its diff:
```python
import functools
import math

import jax
import jax.numpy as jnp
from jax import lax
from jax.experimental import pallas as pl
from jax.experimental.pallas import tpu as pltpu
from jax.sharding import PartitionSpec as P

MESH = pl.DeviceIdType.MESH
NZ, NY, NX = 16, 4, 4
D = 1024
FR = 512
PH = 64
RADIUS = 32.0
WIN = 128
KEYS = FR + 2 * WIN
BLK = 128
SPAN = BLK + 2 * WIN
GROUP = 256
SCALE = math.log2(math.e) / 8.0
QRY, KEY, VAL, OUT = 0, 1, 2, 3


def kernel(ph, spread, dur, gain, w_qry, w_key, w_val, w_out, out,
           wb, wo, phx, phall, gall, sent, pall, aux, auxs, up, qs, ks, vs, probs, att,
           zs, zr, ms, mr, ls, lr, cs, cr, own, xs, xr, ps, pr, es, er, hs, hr, asem, arem):
    s = lax.axis_index("seq")
    d = lax.axis_index("dp")
    z, y, x, c = s // NY, s % NY, d // 2, d % 2
    shards = (w_qry, w_key, w_val, w_out)
    blocks = NZ * NY

    def at(dz, dy, dx, dc):
        zz, yy, xx, cc = (z + dz) % NZ, (y + dy) % NY, (x + dx) % NX, (c + dc) % 2
        return (zz * NY + yy, xx * 2 + cc)

    def beside(step, j):
        return ((s + blocks + step) % blocks, (d + j) % 8)

    barrier = pltpu.get_barrier_semaphore()

    def greet(dev):
        pl.semaphore_signal(barrier, inc=1, device_id=dev, device_id_type=MESH)

    for k in range(1, NZ):
        greet(at(k, 0, 0, 0))
    for k in range(1, NY):
        greet(at(0, k, 0, 0))
    for j in range(8):
        if j:
            greet(beside(0, j))
        greet(beside(1, j))
        greet(beside(-1, j))

    durf = dur[...].astype(jnp.float32)
    row = lax.broadcasted_iota(jnp.int32, (PH, PH), 0)
    col = lax.broadcasted_iota(jnp.int32, (PH, PH), 1)
    tri = jnp.where(row <= col, 1.0, 0.0).astype(jnp.bfloat16)
    ends = jnp.dot(jnp.broadcast_to(durf, (8, PH)).astype(jnp.bfloat16), tri,
                   preferred_element_type=jnp.float32)
    auxs[...] = jnp.zeros_like(auxs)
    auxs[0:1, 0:PH] = ends[0:1] - durf * 0.5
    auxs[1:2, 0:PH] = spread[...]
    aux[1] = auxs[...]

    pl.semaphore_wait(barrier, (NZ - 1) + (NY - 1) + 7 + 16)

    def remote(src, dst, ssem, rsem, dev):
        return pltpu.make_async_remote_copy(
            src_ref=src, dst_ref=dst, send_sem=ssem, recv_sem=rsem, device_id=dev, device_id_type=MESH)

    def waited(ref, sem):
        pltpu.make_async_copy(ref, ref, sem).wait()

    columns = pl.ds(pl.multiple_of(d * 128, 128), 128)

    def place(w):
        return wo.at[x, c, z, y] if w == OUT else wb.at[w, z, y]

    def start_z(w):
        piece = shards[w].at[:, columns]
        pltpu.make_async_copy(piece, place(w), own.at[w]).start()

        def send_z(j, carry):
            half = (j + 1) // 2
            k = 8 + half * (1 - 2 * (j % 2))
            remote(piece, place(w), zs.at[w], zr.at[w], at(k, 0, 0, 0)).start()
            return carry

        lax.fori_loop(0, NZ - 1, send_z, 0)

    start_z(QRY)
    remote(auxs, aux.at[0], asem.at[0], arem.at[0], beside(1, 0)).start()
    remote(auxs, aux.at[2], asem.at[1], arem.at[1], beside(-1, 0)).start()
    remote(ph, phx.at[0], hs.at[0], hr.at[0], beside(1, 0)).start()
    remote(ph, phx.at[2], hs.at[1], hr.at[1], beside(-1, 0)).start()
    for k in (1, 3, 2):
        remote(ph, phall.at[d], xs.at[0], xr.at[k - 1], at(0, 0, k, 0)).start()
    remote(ph, phall.at[d], ps.at[0], pr.at[0], at(0, 0, 0, 1)).start()
    pltpu.make_async_copy(ph, phall.at[d], own.at[4]).start()
    pltpu.make_async_copy(ph, phx.at[1], own.at[5]).start()
    start_z(KEY)
    start_z(VAL)
    start_z(OUT)

    def share():
        for k in (1, 3, 2):
            got = phall.at[((x + NX - k) % NX) * 2 + c]
            waited(got, xr.at[k - 1])
            remote(got, got, ps.at[0], pr.at[0], at(0, 0, 0, 1)).start()

    def mid(w):
        pltpu.make_async_copy(shards[w].at[:, columns], place(w), own.at[w]).wait()
        if w == OUT:
            waited(wo.at[x, c, pl.ds(0, NZ - 1), 0], zr.at[w])
            plane, dy, dx = wo.at[x, c, :, y], 1 - c, c
        else:
            waited(wb.at[w, pl.ds(0, NZ - 1), 0], zr.at[w])
            plane, dy, dx = wb.at[w, :, y], 1, 0
        for k in (2, 1, 3):
            remote(plane, plane, ms.at[w], mr.at[w], at(0, k * dy, k * dx, 0)).start()

    def portion(cc, k):
        if cc == 0:
            return wo.at[(x + NX - k) % NX, 0]
        return wo.at[:, 1, :, (y + NY - k) % NY]

    def each_core(body):
        for cc in range(2):
            pl.when(c == cc)(functools.partial(body, cc))

    def to_partner(ref):
        remote(ref, ref, cs.at[0], cr.at[0], at(0, 0, 0, 1)).start()

    def last():
        waited(wo.at[x, c, pl.ds(0, 12)], mr.at[OUT])

        def body(cc):
            mine = portion(cc, 0)
            for k in (1, 3, 2):
                remote(mine, mine, ls.at[0], lr.at[k - 1], at(0, k * cc, k * (1 - cc), 0)).start()
            to_partner(mine)

        each_core(body)

    def swap():
        def body(cc):
            for k in (1, 3, 2):
                waited(portion(cc, k), lr.at[k - 1])
                to_partner(portion(cc, k))

        each_core(body)

    def whole():
        waited(wo.at[:, 0], cr.at[0])

    def gather_phonemes():
        pltpu.make_async_copy(ph, phall.at[d], own.at[4]).wait()
        waited(phall.at[pl.ds(0, 4)], pr.at[0])
        for i in range(8):
            gall[i] = (phall[i].astype(jnp.float32) * gain[...]).astype(jnp.bfloat16)

    def deliver(w):
        waited(wb.at[w, pl.ds(0, 12)], mr.at[w])
        made = jnp.dot(gall[...].reshape(8 * PH, D), wb[w].reshape(D, 128), preferred_element_type=jnp.float32)
        sent[w] = made.astype(jnp.bfloat16).reshape(8, PH, 128)
        pltpu.make_async_copy(sent.at[w, d], pall.at[w, 1, d], own.at[6 + w]).start()

        def near(j, carry):
            remote(sent.at[w, (d + j) % 8], pall.at[w, 1, d], es.at[2 * w], er.at[2 * w], beside(0, j)).start()
            return carry

        def far(j, carry):
            mine = sent.at[w, (d + j) % 8]
            remote(mine, pall.at[w, 0, d], es.at[2 * w + 1], er.at[2 * w + 1], beside(1, j)).start()
            remote(mine, pall.at[w, 2, d], es.at[2 * w + 1], er.at[2 * w + 1], beside(-1, j)).start()
            return carry

        lax.fori_loop(0, 8, far, 0)
        lax.fori_loop(1, 8, near, 0)

    def upsample():
        waited(aux.at[0], arem.at[0])
        waited(aux.at[2], arem.at[1])
        cent = jnp.concatenate(
            [aux[0, 0:1, 0:PH] - FR, aux[1, 0:1, 0:PH], aux[2, 0:1, 0:PH] + FR], axis=1)
        sig = jnp.concatenate(
            [aux[0, 1:2, 0:PH], aux[1, 1:2, 0:PH], aux[2, 1:2, 0:PH]], axis=1)
        slot = lax.broadcasted_iota(jnp.int32, (1, 3 * PH), 1)
        usable = ((slot >= PH) | (s > 0)) & ((slot < 2 * PH) | (s < blocks - 1))
        reach = jnp.where(usable, RADIUS, -1.0)
        fall = -0.5 / (sig * sig)
        frame = lax.broadcasted_iota(jnp.int32, (KEYS, 3 * PH), 0).astype(jnp.float32) + (0.5 - WIN)
        gap = frame - cent
        band = jnp.where(jnp.abs(gap) <= reach, jnp.exp(gap * gap * fall), 0.0)
        total = jnp.sum(band, axis=1, keepdims=True)
        inv = jnp.where(total > 1e-16, 1.0 / total, 0.0)
        band_bf = band.astype(jnp.bfloat16)
        waited(phx.at[0], hr.at[0])
        waited(phx.at[2], hr.at[1])
        pltpu.make_async_copy(ph, phx.at[1], own.at[5]).wait()
        rows = phx[...].reshape(3 * PH, D)
        lifted = (jnp.dot(band_bf, rows, preferred_element_type=jnp.float32) * inv).astype(jnp.bfloat16)
        up[...] = lifted[WIN:WIN + FR]
        wide = lifted.astype(jnp.float32)
        norm = lax.rsqrt(jnp.mean(wide * wide, axis=1, keepdims=True) + 1e-6) * inv
        return band_bf, norm

    def project(w, band_rows, scale, dest):
        waited(pall.at[w, pl.ds(0, 2)], er.at[2 * w + 1])
        waited(pall.at[w, 0, pl.ds(0, 7)], er.at[2 * w])
        pltpu.make_async_copy(sent.at[w, d], pall.at[w, 1, d], own.at[6 + w]).wait()
        for g in range(4):
            part = jnp.concatenate(
                [pall[w, :, 2 * g].reshape(3 * PH, 128), pall[w, :, 2 * g + 1].reshape(3 * PH, 128)], axis=1)
            dest[:, g * GROUP:(g + 1) * GROUP] = (
                jnp.dot(band_rows, part, preferred_element_type=jnp.float32) * scale).astype(jnp.bfloat16)

    t_id = lax.broadcasted_iota(jnp.int32, (BLK, BLK), 0)
    u_id = lax.broadcasted_iota(jnp.int32, (BLK, BLK), 1)
    lane = lax.broadcasted_iota(jnp.int32, (BLK, GROUP), 1) // 64
    low = -1e30

    def weigh(g):
        lanes = slice(g * GROUP, (g + 1) * GROUP)
        for b in range(4):
            q4 = qs[b * BLK:(b + 1) * BLK, lanes]
            k4 = ks[b * BLK:b * BLK + SPAN, lanes]
            head = u_id >= t_id
            tail = u_id <= t_id
            if b == 0:
                head = head & (s > 0)
            if b == 3:
                tail = tail & (s < blocks - 1)
            head = jnp.where(head, 0.0, low)
            tail = jnp.where(tail, 0.0, low)
            stacked = jnp.concatenate([jnp.where(lane == h, q4, jnp.zeros_like(q4)) for h in range(4)], axis=0)
            scores = lax.dot_general(stacked, k4, (((1,), (1,)), ((), ())), preferred_element_type=jnp.float32)
            bias = jnp.concatenate([head, jnp.zeros((BLK, BLK), jnp.float32), tail], axis=1)
            scores = scores + jnp.concatenate([bias] * 4, axis=0)
            raised = jnp.exp2(scores - jnp.max(scores, axis=1, keepdims=True))
            scale = 1.0 / jnp.sum(raised, axis=1, keepdims=True)
            probs[g, b] = (raised * scale).astype(jnp.bfloat16)

    def mix(g):
        lanes = slice(g * GROUP, (g + 1) * GROUP)
        for b in range(4):
            v4 = vs[b * BLK:b * BLK + SPAN, lanes]
            mixed = jnp.dot(probs[g, b], v4, preferred_element_type=jnp.float32)
            got = jnp.zeros((BLK, GROUP), jnp.float32)
            for h in range(4):
                got = jnp.where(lane == h, mixed[h * BLK:(h + 1) * BLK], got)
            att[b * BLK:(b + 1) * BLK, lanes] = got.astype(jnp.bfloat16)

    def finish():
        for g in range(4):
            lanes = slice(g * GROUP, (g + 1) * GROUP)
            weight = jnp.concatenate(
                [wo[g, 0].reshape(D, 128), wo[g, 1].reshape(D, 128)], axis=1)
            out[:, lanes] = (
                jnp.dot(att[...], weight, preferred_element_type=jnp.float32)
                + up[:, lanes].astype(jnp.float32)).astype(jnp.bfloat16)

    share()
    mid(QRY)
    gather_phonemes()
    mid(KEY)
    deliver(QRY)
    mid(VAL)
    band_bf, norm = upsample()
    deliver(KEY)
    mid(OUT)
    deliver(VAL)
    last()
    project(QRY, band_bf[WIN:WIN + FR], norm[WIN:WIN + FR] * SCALE, qs)
    project(KEY, band_bf, norm, ks)
    weigh(0)
    weigh(1)
    swap()
    weigh(2)
    weigh(3)
    project(VAL, band_bf, norm, vs)
    for g in range(4):
        mix(g)
    whole()
    finish()

    for i in range(2):
        waited(auxs, asem.at[i])
        waited(ph, hs.at[i])
    waited(phall.at[pl.ds(0, 3)], xs.at[0])
    waited(phall.at[pl.ds(0, 4)], ps.at[0])
    for w in range(4):
        waited(wo.at[x, c, pl.ds(0, NZ - 1), 0], zs.at[w])
        waited(wo.at[x, c, pl.ds(0, 12)], ms.at[w])
    for w in range(3):
        waited(pall.at[w, 0, pl.ds(0, 7)], es.at[2 * w])
        waited(pall.at[w, pl.ds(0, 2)], es.at[2 * w + 1])
    waited(wo.at[pl.ds(0, 3), c], ls.at[0])
    waited(wo.at[:, c], cs.at[0])


def on_device(phonemes, spread, durations, norm_gain, w_query, w_key, w_value, w_out):
    vmem = pl.BlockSpec(memory_space=pltpu.VMEM)
    hbm = pl.BlockSpec(memory_space=pl.ANY)
    bf = jnp.bfloat16
    f32 = jnp.float32
    dma = pltpu.SemaphoreType.DMA
    return pl.pallas_call(
        kernel,
        out_shape=jax.ShapeDtypeStruct((FR, D), bf),
        in_specs=[hbm, vmem, vmem, vmem, hbm, hbm, hbm, hbm],
        out_specs=vmem,
        scratch_shapes=[
            pltpu.VMEM((3, NZ, NY, 16, 128), bf),
            pltpu.VMEM((NX, 2, NZ, NY, 16, 128), bf),
            pltpu.VMEM((3, PH, D), bf),
            pltpu.VMEM((8, PH, D), bf),
            pltpu.VMEM((8, PH, D), bf),
            pltpu.VMEM((3, 8, PH, 128), bf),
            pltpu.VMEM((3, 3, 8, PH, 128), bf),
            pltpu.VMEM((3, 8, 128), f32),
            pltpu.VMEM((8, 128), f32),
            pltpu.VMEM((FR, D), bf),
            pltpu.VMEM((FR, D), bf),
            pltpu.VMEM((KEYS, D), bf),
            pltpu.VMEM((KEYS, D), bf),
            pltpu.VMEM((4, 4, 4 * BLK, SPAN), bf),
            pltpu.VMEM((FR, D), bf),
            dma((4,)), dma((4,)), dma((4,)), dma((4,)), dma((1,)), dma((3,)),
            dma((1,)), dma((1,)), dma((9,)), dma((1,)), dma((3,)), dma((1,)), dma((1,)),
            dma((6,)), dma((6,)), dma((2,)), dma((2,)), dma((2,)), dma((2,)),
        ],
        compiler_params=pltpu.CompilerParams(
            collective_id=0, has_side_effects=True, vmem_limit_bytes=56 * 1024 * 1024),
        name="chapter_block",
    )(phonemes, spread.reshape(1, PH), durations, norm_gain.reshape(1, D),
      w_query, w_key, w_value, w_out)


def solution(mesh):
    placed = (
        P(("dp", "seq"), None),
        P(("dp", "seq")),
        P(("dp", "seq"), None),
        P(),
        P("seq", None),
        P("seq", None),
        P("seq", None),
        P("seq", None),
    )
    return jax.shard_map(
        on_device, mesh=mesh, in_specs=placed, out_specs=P(("dp", "seq"), None), check_vma=False
    )
```

time: 71.9 us -> 65.6 us (0.912)
  the two profiles are of different devices: /device:TPU:1 before, /device:TPU:154 now
where the time goes in v2:
time: 65.6 us; the launch traced here: 65.4 us
  Pallas kernels  63.1 us (96%)
  local copies, waits for them, and re-layouts  2.26 us (3%)
    pallas_call x1, Pallas kernels, on_device(): pl.pallas_call(kernel, out_shape=jax.ShapeDtypeStruct((FR, D), bf), in_sp...  63.1 us
    unnamed x1, local copies, waits for them, and re-layouts  2.26 us

profile of v2, /device:TPU:154, one launch (start us, length us, event | category | flops | bytes accessed | tf_op | source)
XLA Modules:
  0.0 65.4 jit_solution(6176900298604398071)
XLA Ops:
  0.0 63.1 %chapter_block.1 = bf16[512,1024]{1,0:T(8,128)(2,1)} custom-call(bf16[64,1024]{1,0:T(8,128)(2,1)} %ph.1, f32[1,64]{1,0:T(1,128)} %bitcast.3, s32[1,64]{1,0:T(1,128)} %dur.1, f32[1,1024]{1,0:T(1,128)} %bitcast.2, bf16[16,1024]{1,0:T(8,128)(2,1)} %w_qry.1, bf16[16,1024]{1,0:T(8,128)(2,1)} %w_key.1, bf16[16,1024]{1,0:T(8,128)(2,1)} %w_val.1, bf16[16,1024]{1,0:T(8,128)(2,1)} %w_out.1), custom_call_target="tpu_custom_call" | custom-call | tf_op jit(solution)/shard_map/chapter_block/pallas_call | solution.py:311
  63.1 2.3 %copy.10 = bf16[512,1024]{1,0:T(8,128)(2,1)} copy(bf16[512,1024]{1,0:T(8,128)(2,1)} %chapter_block.1) | data formatting | bytes 2097152

commit v3 on v2

--- a/solution.py
+++ b/solution.py
@@ -1,4 +1,3 @@
-import functools
 import math
 
 import jax
@@ -39,6 +38,20 @@
     def beside(step, j):
         return ((s + blocks + step) % blocks, (d + j) % 8)
 
+    columns = pl.ds(pl.multiple_of(d * 128, 128), 128)
+
+    zh, zl = z // 4, z % 4
+    low, high = pl.ds(0, 2), pl.ds(2, 2)
+    mine = 2 + x % 2
+    local = [pltpu.make_async_copy(shards[w].at[:, columns], wb.at[w, z, y], own.at[w]) for w in range(3)]
+    for i, g in enumerate((0, 1, mine)):
+        part = pl.ds(pl.multiple_of(g * GROUP + c * 128, 128), 128)
+        local.append(pltpu.make_async_copy(w_out.at[:, part], wo.at[g, c, zh, zl, y], own.at[9 + i]))
+    local.append(pltpu.make_async_copy(ph, phall.at[d], own.at[4]))
+    local.append(pltpu.make_async_copy(ph, phx.at[1], own.at[5]))
+    for copy in local:
+        copy.start()
+
     barrier = pltpu.get_barrier_semaphore()
 
     def greet(dev):
@@ -65,6 +78,10 @@
     auxs[1:2, 0:PH] = spread[...]
     aux[1] = auxs[...]
 
+    pall[QRY, 0, :, 0:PH // 2] = jnp.zeros((8, PH // 2, 128), jnp.bfloat16)
+    pall[QRY, 2, :, PH // 2:] = jnp.zeros((8, PH // 2, 128), jnp.bfloat16)
+    for copy in local:
+        copy.wait()
     pl.semaphore_wait(barrier, (NZ - 1) + (NY - 1) + 7 + 16)
 
     def remote(src, dst, ssem, rsem, dev):
@@ -74,34 +91,22 @@
     def waited(ref, sem):
         pltpu.make_async_copy(ref, ref, sem).wait()
 
-    columns = pl.ds(pl.multiple_of(d * 128, 128), 128)
-
-    def place(w):
-        return wo.at[x, c, z, y] if w == OUT else wb.at[w, z, y]
-
     def start_z(w):
-        piece = shards[w].at[:, columns]
-        pltpu.make_async_copy(piece, place(w), own.at[w]).start()
-
-        def send_z(j, carry):
-            half = (j + 1) // 2
-            k = 8 + half * (1 - 2 * (j % 2))
-            remote(piece, place(w), zs.at[w], zr.at[w], at(k, 0, 0, 0)).start()
-            return carry
-
-        lax.fori_loop(0, NZ - 1, send_z, 0)
-
+        piece = wo.at[mine, c, zh, zl, y] if w == OUT else wb.at[w, z, y]
+        for k in (8, 7, 9, 6, 10, 5, 11, 4, 12, 3, 13, 2, 14, 1, 15):
+            remote(piece, piece, zs.at[w], zr.at[w], at(k, 0, 0, 0)).start()
+
+    for k in (2, 1, 3):
+        remote(wo.at[low, c, zh, zl, y], wo.at[low, c, zh, zl, y], ls.at[0], lr.at[0], at(0, k, 0, 0)).start()
     start_z(QRY)
+    for k in (1, 3, 2):
+        remote(phall.at[d], phall.at[d], xs.at[0], xr.at[k - 1], at(0, 0, k, 0)).start()
     remote(auxs, aux.at[0], asem.at[0], arem.at[0], beside(1, 0)).start()
     remote(auxs, aux.at[2], asem.at[1], arem.at[1], beside(-1, 0)).start()
-    remote(ph, phx.at[0], hs.at[0], hr.at[0], beside(1, 0)).start()
-    remote(ph, phx.at[2], hs.at[1], hr.at[1], beside(-1, 0)).start()
-    for k in (1, 3, 2):
-        remote(ph, phall.at[d], xs.at[0], xr.at[k - 1], at(0, 0, k, 0)).start()
-    remote(ph, phall.at[d], ps.at[0], pr.at[0], at(0, 0, 0, 1)).start()
-    pltpu.make_async_copy(ph, phall.at[d], own.at[4]).start()
-    pltpu.make_async_copy(ph, phx.at[1], own.at[5]).start()
+    remote(phall.at[d], phx.at[0], hs.at[0], hr.at[0], beside(1, 0)).start()
+    remote(phall.at[d], phx.at[2], hs.at[1], hr.at[1], beside(-1, 0)).start()
     start_z(KEY)
+    remote(phall.at[d], phall.at[d], ps.at[0], pr.at[0], at(0, 0, 0, 1)).start()
     start_z(VAL)
     start_z(OUT)
 
@@ -112,55 +117,57 @@
             remote(got, got, ps.at[0], pr.at[0], at(0, 0, 0, 1)).start()
 
     def mid(w):
-        pltpu.make_async_copy(shards[w].at[:, columns], place(w), own.at[w]).wait()
-        if w == OUT:
-            waited(wo.at[x, c, pl.ds(0, NZ - 1), 0], zr.at[w])
-            plane, dy, dx = wo.at[x, c, :, y], 1 - c, c
-        else:
-            waited(wb.at[w, pl.ds(0, NZ - 1), 0], zr.at[w])
-            plane, dy, dx = wb.at[w, :, y], 1, 0
+        waited(wb.at[w, pl.ds(0, NZ - 1), 0], zr.at[w])
         for k in (2, 1, 3):
-            remote(plane, plane, ms.at[w], mr.at[w], at(0, k * dy, k * dx, 0)).start()
-
-    def portion(cc, k):
-        if cc == 0:
-            return wo.at[(x + NX - k) % NX, 0]
-        return wo.at[:, 1, :, (y + NY - k) % NY]
-
-    def each_core(body):
-        for cc in range(2):
-            pl.when(c == cc)(functools.partial(body, cc))
-
-    def to_partner(ref):
-        remote(ref, ref, cs.at[0], cr.at[0], at(0, 0, 0, 1)).start()
-
-    def last():
-        waited(wo.at[x, c, pl.ds(0, 12)], mr.at[OUT])
-
-        def body(cc):
-            mine = portion(cc, 0)
-            for k in (1, 3, 2):
-                remote(mine, mine, ls.at[0], lr.at[k - 1], at(0, k * cc, k * (1 - cc), 0)).start()
-            to_partner(mine)
-
-        each_core(body)
-
-    def swap():
-        def body(cc):
-            for k in (1, 3, 2):
-                waited(portion(cc, k), lr.at[k - 1])
-                to_partner(portion(cc, k))
-
-        each_core(body)
+            remote(wb.at[w, :, y], wb.at[w, :, y], ms.at[w], mr.at[w], at(0, k, 0, 0)).start()
+
+    def out_far():
+        waited(wo.at[low, c, zh, zl, pl.ds(0, 3)], lr.at[0])
+        ref = wo.at[low, c, zh, zl]
+        for k in (8, 4, 12):
+            remote(ref, ref, ls.at[1], lr.at[1], at(k, 0, 0, 0)).start()
+
+    def out_near():
+        waited(wo.at[low, c, pl.ds(0, 3), zl], lr.at[1])
+        ref = wo.at[low, c, :, zl]
+        for k in (2, 1, 15):
+            remote(ref, ref, ls.at[2], lr.at[2], at(k, 0, 0, 0)).start()
+
+    def out_pair():
+        waited(wb.at[0, pl.ds(0, NZ - 1), 0], zr.at[OUT])
+        ref = wo.at[mine, c, :, :, y]
+        remote(ref, ref, ms.at[OUT], mr.at[OUT], at(0, 0, 1 + 2 * (x % 2), 0)).start()
+
+    def out_plane():
+        waited(wo.at[5 - mine, c, :, :, y], mr.at[OUT])
+        ref = wo.at[high, c, :, :, y]
+        for k in (2, 1, 3):
+            remote(ref, ref, ls.at[3], lr.at[3], at(0, k, 0, 0)).start()
+
+    def swap_low():
+        waited(wo.at[low, c, :, pl.ds(0, 3)], lr.at[2])
+        remote(wo.at[low, c], wo.at[low, c], cs.at[0], cr.at[0], at(0, 0, 0, 1)).start()
+
+    def swap_high():
+        waited(wo.at[high, c, :, :, pl.ds(0, 3)], lr.at[3])
+        remote(wo.at[high, c], wo.at[high, c], cs.at[1], cr.at[1], at(0, 0, 0, 1)).start()
 
     def whole():
-        waited(wo.at[:, 0], cr.at[0])
+        waited(wo.at[low, 1 - c], cr.at[0])
+        waited(wo.at[high, 1 - c], cr.at[1])
 
     def gather_phonemes():
-        pltpu.make_async_copy(ph, phall.at[d], own.at[4]).wait()
         waited(phall.at[pl.ds(0, 4)], pr.at[0])
         for i in range(8):
             gall[i] = (phall[i].astype(jnp.float32) * gain[...]).astype(jnp.bfloat16)
+
+    def reach_of(w):
+        if w == QRY:
+            return slice(PH // 2, PH), slice(0, PH // 2)
+        return slice(0, PH), slice(0, PH)
+
+    def far_bytes(w):
+        return pall.at[w, 0] if w == QRY else pall.at[w, pl.ds(0, 2)]
 
     def deliver(w):
         waited(wb.at[w, pl.ds(0, 12)], mr.at[w])
@@ -172,10 +179,12 @@
             remote(sent.at[w, (d + j) % 8], pall.at[w, 1, d], es.at[2 * w], er.at[2 * w], beside(0, j)).start()
             return carry
 
+        late, early = reach_of(w)
+
         def far(j, carry):
             mine = sent.at[w, (d + j) % 8]
-            remote(mine, pall.at[w, 0, d], es.at[2 * w + 1], er.at[2 * w + 1], beside(1, j)).start()
-            remote(mine, pall.at[w, 2, d], es.at[2 * w + 1], er.at[2 * w + 1], beside(-1, j)).start()
+            remote(mine.at[late], pall.at[w, 0, d, late], es.at[2 * w + 1], er.at[2 * w + 1], beside(1, j)).start()
+            remote(mine.at[early], pall.at[w, 2, d, early], es.at[2 * w + 1], er.at[2 * w + 1], beside(-1, j)).start()
             return carry
 
         lax.fori_loop(0, 8, far, 0)
@@ -200,7 +209,6 @@
         band_bf = band.astype(jnp.bfloat16)
         waited(phx.at[0], hr.at[0])
         waited(phx.at[2], hr.at[1])
-        pltpu.make_async_copy(ph, phx.at[1], own.at[5]).wait()
         rows = phx[...].reshape(3 * PH, D)
         lifted = (jnp.dot(band_bf, rows, preferred_element_type=jnp.float32) * inv).astype(jnp.bfloat16)
         up[...] = lifted[WIN:WIN + FR]
@@ -209,7 +217,7 @@
         return band_bf, norm
 
     def project(w, band_rows, scale, dest):
-        waited(pall.at[w, pl.ds(0, 2)], er.at[2 * w + 1])
+        waited(far_bytes(w), er.at[2 * w + 1])
         waited(pall.at[w, 0, pl.ds(0, 7)], er.at[2 * w])
         pltpu.make_async_copy(sent.at[w, d], pall.at[w, 1, d], own.at[6 + w]).wait()
         for g in range(4):
@@ -221,7 +229,7 @@
     t_id = lax.broadcasted_iota(jnp.int32, (BLK, BLK), 0)
     u_id = lax.broadcasted_iota(jnp.int32, (BLK, BLK), 1)
     lane = lax.broadcasted_iota(jnp.int32, (BLK, GROUP), 1) // 64
-    low = -1e30
+    never = -1e30
 
     def weigh(g):
         lanes = slice(g * GROUP, (g + 1) * GROUP)
@@ -234,8 +242,8 @@
                 head = head & (s > 0)
             if b == 3:
                 tail = tail & (s < blocks - 1)
-            head = jnp.where(head, 0.0, low)
-            tail = jnp.where(tail, 0.0, low)
+            head = jnp.where(head, 0.0, never)
+            tail = jnp.where(tail, 0.0, never)
             stacked = jnp.concatenate([jnp.where(lane == h, q4, jnp.zeros_like(q4)) for h in range(4)], axis=0)
             scores = lax.dot_general(stacked, k4, (((1,), (1,)), ((), ())), preferred_element_type=jnp.float32)
             bias = jnp.concatenate([head, jnp.zeros((BLK, BLK), jnp.float32), tail], axis=1)
@@ -263,22 +271,25 @@
                 jnp.dot(att[...], weight, preferred_element_type=jnp.float32)
                 + up[:, lanes].astype(jnp.float32)).astype(jnp.bfloat16)
 
+    out_far()
+    mid(QRY)
+    mid(KEY)
     share()
-    mid(QRY)
+    mid(VAL)
     gather_phonemes()
-    mid(KEY)
     deliver(QRY)
-    mid(VAL)
+    out_pair()
+    deliver(KEY)
+    deliver(VAL)
+    out_plane()
+    out_near()
     band_bf, norm = upsample()
-    deliver(KEY)
-    mid(OUT)
-    deliver(VAL)
-    last()
     project(QRY, band_bf[WIN:WIN + FR], norm[WIN:WIN + FR] * SCALE, qs)
     project(KEY, band_bf, norm, ks)
     weigh(0)
     weigh(1)
-    swap()
+    swap_high()
+    swap_low()
     weigh(2)
     weigh(3)
     project(VAL, band_bf, norm, vs)
@@ -289,17 +300,22 @@
 
     for i in range(2):
         waited(auxs, asem.at[i])
-        waited(ph, hs.at[i])
+        waited(phx.at[1], hs.at[i])
     waited(phall.at[pl.ds(0, 3)], xs.at[0])
     waited(phall.at[pl.ds(0, 4)], ps.at[0])
     for w in range(4):
-        waited(wo.at[x, c, pl.ds(0, NZ - 1), 0], zs.at[w])
-        waited(wo.at[x, c, pl.ds(0, 12)], ms.at[w])
+        waited(wb.at[0, pl.ds(0, NZ - 1), 0], zs.at[w])
     for w in range(3):
+        waited(wb.at[w, pl.ds(0, 12)], ms.at[w])
         waited(pall.at[w, 0, pl.ds(0, 7)], es.at[2 * w])
-        waited(pall.at[w, pl.ds(0, 2)], es.at[2 * w + 1])
-    waited(wo.at[pl.ds(0, 3), c], ls.at[0])
-    waited(wo.at[:, c], cs.at[0])
+        waited(far_bytes(w), es.at[2 * w + 1])
+    waited(wo.at[mine, c, :, :, y], ms.at[OUT])
+    waited(wo.at[low, c, zh, zl, pl.ds(0, 3)], ls.at[0])
+    waited(wo.at[low, c, pl.ds(0, 3), zl], ls.at[1])
+    waited(wo.at[low, c, :, pl.ds(0, 3)], ls.at[2])
+    waited(wo.at[high, c, :, :, pl.ds(0, 3)], ls.at[3])
+    waited(wo.at[low, c], cs.at[0])
+    waited(wo.at[high, c], cs.at[1])
 
 
 def on_device(phonemes, spread, durations, norm_gain, w_query, w_key, w_value, w_out):
@@ -315,7 +331,7 @@
         out_specs=vmem,
         scratch_shapes=[
             pltpu.VMEM((3, NZ, NY, 16, 128), bf),
-            pltpu.VMEM((NX, 2, NZ, NY, 16, 128), bf),
+            pltpu.VMEM((4, 2, 4, 4, NY, 16, 128), bf),
             pltpu.VMEM((3, PH, D), bf),
             pltpu.VMEM((8, PH, D), bf),
             pltpu.VMEM((8, PH, D), bf),
@@ -329,8 +345,8 @@
             pltpu.VMEM((KEYS, D), bf),
             pltpu.VMEM((4, 4, 4 * BLK, SPAN), bf),
             pltpu.VMEM((FR, D), bf),
-            dma((4,)), dma((4,)), dma((4,)), dma((4,)), dma((1,)), dma((3,)),
-            dma((1,)), dma((1,)), dma((9,)), dma((1,)), dma((3,)), dma((1,)), dma((1,)),
+            dma((4,)), dma((4,)), dma((4,)), dma((4,)), dma((4,)), dma((4,)),
+            dma((2,)), dma((2,)), dma((12,)), dma((1,)), dma((3,)), dma((1,)), dma((1,)),
             dma((6,)), dma((6,)), dma((2,)), dma((2,)), dma((2,)), dma((2,)),
         ],
         compiler_params=pltpu.CompilerParams(

time: 65.6 us -> 62.6 us (0.954)
  the two profiles are of different devices: /device:TPU:154 before, /device:TPU:2 now
where the time goes in v3:
time: 62.6 us; the launch traced here: 62.4 us
  Pallas kernels  60.2 us (96%)
  local copies, waits for them, and re-layouts  2.26 us (4%)
    pallas_call x1, Pallas kernels, on_device(): pl.pallas_call(kernel, out_shape=jax.ShapeDtypeStruct((FR, D), bf), in_sp...  60.2 us
    unnamed x1, local copies, waits for them, and re-layouts  2.26 us

profile of v3, /device:TPU:2, one launch (start us, length us, event | category | flops | bytes accessed | tf_op | source)
XLA Modules:
  0.0 62.4 jit_solution(2617991743799160779)
XLA Ops:
  0.0 60.2 %chapter_block.1 = bf16[512,1024]{1,0:T(8,128)(2,1)} custom-call(bf16[64,1024]{1,0:T(8,128)(2,1)} %ph.1, f32[1,64]{1,0:T(1,128)} %bitcast.3, s32[1,64]{1,0:T(1,128)} %dur.1, f32[1,1024]{1,0:T(1,128)} %bitcast.2, bf16[16,1024]{1,0:T(8,128)(2,1)} %w_qry.1, bf16[16,1024]{1,0:T(8,128)(2,1)} %w_key.1, bf16[16,1024]{1,0:T(8,128)(2,1)} %w_val.1, bf16[16,1024]{1,0:T(8,128)(2,1)} %w_out.1), custom_call_target="tpu_custom_call" | custom-call | tf_op jit(solution)/shard_map/chapter_block/pallas_call | solution.py:327
  60.2 2.3 %copy.10 = bf16[512,1024]{1,0:T(8,128)(2,1)} copy(bf16[512,1024]{1,0:T(8,128)(2,1)} %chapter_block.1) | data formatting | bytes 2097152

commit v4 on v3

--- a/solution.py
+++ b/solution.py
@@ -152,9 +152,8 @@
         waited(wo.at[high, c, :, :, pl.ds(0, 3)], lr.at[3])
         remote(wo.at[high, c], wo.at[high, c], cs.at[1], cr.at[1], at(0, 0, 0, 1)).start()
 
-    def whole():
-        waited(wo.at[low, 1 - c], cr.at[0])
-        waited(wo.at[high, 1 - c], cr.at[1])
+    def whole(part, i):
+        waited(wo.at[part, 1 - c], cr.at[i])
 
     def gather_phonemes():
         waited(phall.at[pl.ds(0, 4)], pr.at[0])
@@ -262,8 +261,8 @@
                 got = jnp.where(lane == h, mixed[h * BLK:(h + 1) * BLK], got)
             att[b * BLK:(b + 1) * BLK, lanes] = got.astype(jnp.bfloat16)
 
-    def finish():
-        for g in range(4):
+    def finish(groups):
+        for g in groups:
             lanes = slice(g * GROUP, (g + 1) * GROUP)
             weight = jnp.concatenate(
                 [wo[g, 0].reshape(D, 128), wo[g, 1].reshape(D, 128)], axis=1)
@@ -288,15 +287,19 @@
     project(KEY, band_bf, norm, ks)
     weigh(0)
     weigh(1)
-    swap_high()
-    swap_low()
     weigh(2)
     weigh(3)
+    swap_high()
     project(VAL, band_bf, norm, vs)
-    for g in range(4):
-        mix(g)
-    whole()
-    finish()
+    mix(0)
+    mix(1)
+    swap_low()
+    mix(2)
+    mix(3)
+    whole(high, 1)
+    finish((2, 3))
+    whole(low, 0)
+    finish((0, 1))
 
     for i in range(2):
         waited(auxs, asem.at[i])

time: 62.6 us -> 61 us (0.974)
  the two profiles are of different devices: /device:TPU:2 before, /device:TPU:1 now
where the time goes in v4:
time: 61 us; the launch traced here: 60.8 us
  Pallas kernels  58.5 us (96%)
  local copies, waits for them, and re-layouts  2.26 us (4%)
    pallas_call x1, Pallas kernels, on_device(): pl.pallas_call(kernel, out_shape=jax.ShapeDtypeStruct((FR, D), bf), in_sp...  58.5 us
    unnamed x1, local copies, waits for them, and re-layouts  2.26 us

profile of v4, /device:TPU:1, one launch (start us, length us, event | category | flops | bytes accessed | tf_op | source)
XLA Modules:
  0.0 60.8 jit_solution(5896353330432145889)
XLA Ops:
  0.0 58.5 %chapter_block.1 = bf16[512,1024]{1,0:T(8,128)(2,1)} custom-call(bf16[64,1024]{1,0:T(8,128)(2,1)} %ph.1, f32[1,64]{1,0:T(1,128)} %bitcast.3, s32[1,64]{1,0:T(1,128)} %dur.1, f32[1,1024]{1,0:T(1,128)} %bitcast.2, bf16[16,1024]{1,0:T(8,128)(2,1)} %w_qry.1, bf16[16,1024]{1,0:T(8,128)(2,1)} %w_key.1, bf16[16,1024]{1,0:T(8,128)(2,1)} %w_val.1, bf16[16,1024]{1,0:T(8,128)(2,1)} %w_out.1), custom_call_target="tpu_custom_call" | custom-call | tf_op jit(solution)/shard_map/chapter_block/pallas_call | solution.py:330
  58.5 2.3 %copy.10 = bf16[512,1024]{1,0:T(8,128)(2,1)} copy(bf16[512,1024]{1,0:T(8,128)(2,1)} %chapter_block.1) | data formatting | bytes 2097152
